TPU v7x, 512 devices: a whole 4x8x8 slice. The times are simulated.
512 devices in a mesh: clip: 16 (over x, y_hi, core), tm: 32 (over y_lo, z).
Axes of the slice: x: 4, y: 8 (y_hi: 2, y_lo: 4; y = y_hi * 4 + y_lo), z: 8, core: 2. Of those that a mesh axis runs over, the one named last changes fastest.
Arguments:
- inputs: bfloat16 [16, 10240, 768], P('clip', 'tm'), may hold values from -6 to 6
- query_states: bfloat16 [16, 10240, 768], P('clip', 'tm'), may hold values from -9 to 9
- key_states: bfloat16 [16, 10240, 768], P('clip', 'tm'), may hold values from -9 to 9
- value_states: bfloat16 [16, 10240, 768], P('clip', 'tm'), may hold values from -6 to 6
- out_grad: bfloat16 [16, 10240, 768], P('clip', 'tm'), may hold values from -1.1953125 to 1.1953125
- first_flags: int32 [16, 32], P('clip'), may hold values from 0 to 1, as said below
- weight: float32 [768, 768], P('tm'), may hold values from -1.2 to 1.2
- moment_one: float32 [768, 768], P('tm'), may hold values from -6 to 6
- moment_two: float32 [768, 768], P('tm'), may hold values from 0.25 to 4
Outputs:
- new_weight: float32 [768, 768], P('tm')
- new_moment_one: float32 [768, 768], P('tm')
- new_moment_two: float32 [768, 768], P('tm')
Inputs may be any that keep to these rules, and one draw needn't show every extreme that they name: `first_flags`: the first frame of every sequence has flag 1.
All inputs are finite; a program needn't handle non-finite values.
Results may differ from a plain program's by a relative error of at most 0.0044.
Values may be sent and summed in bfloat16 or wider, within the bound.
A program may use at most 64 MiB of HBM per device.

v0:
```python
import math

import jax
import jax.numpy as jnp
from jax import lax
from jax.sharding import PartitionSpec as P

HEAD_DIM = 128


beta_one = 0.9
beta_two = 0.95
learn_rate = 0.001
adam_eps = 1e-08
decay_rate = 0.1
step_count = 10.0


def from_behind(value, axis, steps):
    count = lax.axis_size(axis)
    leading, last = (max(0, -steps), min(count, count - steps))
    return lax.ppermute(value, axis, [(source, source + steps) for source in range(leading, last)])


def cut_along(value, dim, length):
    dims = value.shape
    tiles = value.reshape(*dims[:dim], length, dims[dim] // length, *dims[dim + 1 :])
    return jnp.moveaxis(tiles, dim, 0)


def summed_on_arrival(value, axis, dim):
    length = lax.axis_size(axis)
    tiles = lax.all_to_all(cut_along(value, dim, length), axis, 0, 0, tiled=True)
    return jnp.sum(tiles, axis=0)


def copy_for_each(value, axis):
    length = lax.axis_size(axis)
    return lax.all_to_all(
        jnp.broadcast_to(value[None], (length, *value.shape)), axis, 0, 0, tiled=True
    )


def over_copies(value, axis):
    return copy_for_each(value, axis).sum(axis=0)


def adamw(weight, moment_one, moment_two, gradient):
    new_one = beta_one * moment_one + (1.0 - beta_one) * gradient
    new_two = beta_two * moment_two + (1.0 - beta_two) * gradient * gradient
    corr_one = new_one / (1.0 - beta_one**step_count)
    corr_two = new_two / (1.0 - beta_two**step_count)
    new_weight = weight - learn_rate * (
        corr_one / (jnp.sqrt(corr_two) + adam_eps) + decay_rate * weight
    )
    return (new_weight, new_one, new_two)


def window_grad(query_rows, key_window, value_window, grad_rows, allowed):
    tok_rows = query_rows.shape[0]
    head_size = HEAD_DIM
    head_count = query_rows.shape[1] // head_size
    scaling = 1.0 / math.sqrt(head_size)
    query_heads = query_rows.reshape(tok_rows, head_count, head_size)
    key_heads = key_window.reshape(3 * tok_rows, head_count, head_size)
    value_heads = value_window.reshape(3 * tok_rows, head_count, head_size)
    grad_heads = grad_rows.reshape(tok_rows, head_count, head_size)
    scores = (
        jnp.einsum("qhd,khd->hqk", query_heads, key_heads, preferred_element_type=jnp.float32)
        * scaling
    )
    scores = jnp.where(allowed[None, None, :], scores, -jnp.inf)
    row_max = jnp.max(scores, axis=-1, keepdims=True)
    raised = jnp.exp(scores - row_max)
    softmax = raised / jnp.sum(raised, axis=-1, keepdims=True)
    dprobs = jnp.einsum("qhd,khd->hqk", grad_heads, value_heads, preferred_element_type=jnp.float32)
    row_dot = jnp.sum(softmax * dprobs, axis=-1, keepdims=True)
    dscores = (softmax * (dprobs - row_dot) * scaling).astype(jnp.bfloat16)
    window_part = jnp.einsum(
        "hqk,qhd->khd", dscores, query_heads, preferred_element_type=jnp.float32
    )
    return window_part.reshape(3 * tok_rows, head_count * head_size)


def contract_rows(features, key_grad):
    return lax.dot_general(
        features, key_grad, (((0,), (0,)), ((), ())), preferred_element_type=jnp.float32
    )


def body(
    inputs,
    query_states,
    key_states,
    value_states,
    out_grad,
    first_flags,
    weight,
    moment_one,
    moment_two,
):
    tok_rows = inputs.shape[1]
    position = lax.axis_index("tm")
    flag_row = first_flags[0]
    own_flag = flag_row[position]
    prev_flag = jnp.where(position >= 1, flag_row[jnp.maximum(position - 1, 0)], 1)
    near_ok = own_flag == 0
    far_ok = jnp.logical_and(near_ok, prev_flag == 0)
    allowed = jnp.concatenate(
        [
            jnp.broadcast_to(far_ok, (tok_rows,)),
            jnp.broadcast_to(near_ok, (tok_rows,)),
            jnp.ones((tok_rows,), bool),
        ]
    )
    queries = query_states[0]
    keys_own = key_states[0]
    values_own = value_states[0]
    near_keys, near_values = from_behind((keys_own, values_own), "tm", 1)
    far_keys, far_values = from_behind((near_keys, near_values), "tm", 1)
    key_window = jnp.concatenate([far_keys, near_keys, keys_own], axis=0)
    value_window = jnp.concatenate([far_values, near_values, values_own], axis=0)
    window_part = window_grad(queries, key_window, value_window, out_grad[0], allowed)
    far_part = window_part[:tok_rows]
    near_part = window_part[tok_rows : 2 * tok_rows]
    own_part = window_part[2 * tok_rows :]
    carried = from_behind(far_part, "tm", -1)
    returned = from_behind(near_part + carried, "tm", -1)
    summed = own_part + returned
    key_grad = summed.astype(jnp.bfloat16)
    features = inputs[0]
    local_rows = summed_on_arrival(contract_rows(features, key_grad), "tm", 0)
    gradient = over_copies(local_rows, "clip")
    return adamw(weight, moment_one, moment_two, gradient)


def solution(mesh):
    in_specs = (
        P("clip", "tm", None),
        P("clip", "tm", None),
        P("clip", "tm", None),
        P("clip", "tm", None),
        P("clip", "tm", None),
        P("clip", None),
        P("tm", None),
        P("tm", None),
        P("tm", None),
    )
    out_specs = (P("tm", None), P("tm", None), P("tm", None))
    return jax.shard_map(body, mesh=mesh, in_specs=in_specs, out_specs=out_specs, check_vma=False)
```

profile of v0, /device:TPU:9, one launch (start us, length us, event | category | flops | bytes accessed | tf_op | source)
XLA Modules:
  0.0 260.8 jit_solution(11265677189435014490)
XLA Ops:
  0.6 4.1 %collective-permute-start = (bf16[320,768]{1,0:T(8,128)(2,1)}, bf16[320,768]{1,0:T(8,128)(2,1)}, u32[]{:S(2)}, u32[]{:S(2)}) collective-permute-start(bf16[320,768]{1,0:T(8,128)(2,1)} %bitcast.73), channel_id=1, source_target_pairs={{0,1},{1,2},{2,3},{3,4},{4,5},{5,6},{6,7},{7,8},{8,9},{9,10},{10,1... | collective-permute-start | bytes 1474568 | tf_op jit(solution)/shard_map/ppermute | solution.py:22
  4.8 4.0 %collective-permute-start.2 = (bf16[320,768]{1,0:T(8,128)(2,1)}, bf16[320,768]{1,0:T(8,128)(2,1)}, u32[]{:S(2)}, u32[]{:S(2)}) collective-permute-start(bf16[320,768]{1,0:T(8,128)(2,1)} %bitcast.74), channel_id=1, source_target_pairs={{0,1},{1,2},{2,3},{3,4},{4,5},{5,6},{6,7},{7,8},{8,9},{9,10},{10,1... | collective-permute-start | bytes 1474568 | tf_op jit(solution)/shard_map/ppermute | solution.py:22
  8.8 13.8 %collective-permute-done = bf16[320,768]{1,0:T(8,128)(2,1)} collective-permute-done((bf16[320,768]{1,0:T(8,128)(2,1)}, bf16[320,768]{1,0:T(8,128)(2,1)}, u32[]{:S(2)}, u32[]{:S(2)}) %collective-permute-start) | collective-permute-done | bytes 491552 | tf_op jit(solution)/shard_map/ppermute | solution.py:22
  22.6 1.9 collective-permute-start.1
  24.5 8.6 %collective-permute-done.2 = bf16[320,768]{1,0:T(8,128)(2,1)} collective-permute-done((bf16[320,768]{1,0:T(8,128)(2,1)}, bf16[320,768]{1,0:T(8,128)(2,1)}, u32[]{:S(2)}, u32[]{:S(2)}) %collective-permute-start.2) | collective-permute-done | bytes 491552 | tf_op jit(solution)/shard_map/ppermute | solution.py:22
  33.1 1.9 collective-permute-start.3
  35.0 1.3 copy.85
  36.4 1.3 copy.93
  39.7 1.3 copy.89
  41.7 1.3 copy.97
  43.8 1.3 copy.84
  46.1 1.3 copy.92
  48.5 1.3 copy.83
  50.9 3.3 %collective-permute-done.3 = bf16[320,768]{1,0:T(8,128)(2,1)} collective-permute-done((bf16[320,768]{1,0:T(8,128)(2,1)}, bf16[320,768]{1,0:T(8,128)(2,1)}, u32[]{:S(2)}, u32[]{:S(2)}) %collective-permute-start.3) | collective-permute-done | bytes 491552 | tf_op jit(solution)/shard_map/ppermute | solution.py:22
  54.2 1.3 copy.91
  56.6 5.6 %fusion.21 = f32[6,960,320]{1,2,0:T(8,128)} fusion(bf16[320,6,128]{0,2,1:T(8,128)(2,1)S(1)} %bitcast.64, bf16[320,6,128]{2,0,1:T(8,128)(2,1)S(1)} %copy.88, bf16[320,6,128]{2,0,1:T(8,128)(2,1)} %copy.87, bf16[320,6,128]{2,0,1:T(8,128)(2,1)} %copy.86), kind=kOutput, calls=%fused_computation.21 | convolution fusion | flops 476282880 | bytes 9338880 | tf_op jit(solution)/shard_map/qhd,khd->hqk/dot_general | solution.py:69
  62.1 11.5 %fusion.16 = f32[6,320,960]{2,1,0:T(8,128)} fusion(f32[6,960,320]{1,2,0:T(8,128)} %fusion.21, pred[960]{0:T(1024)(128)(4,1)S(1)} %pad_add_fusion), kind=kOutput, calls=%fused_computation.18 | output fusion | flops 11064958 | bytes 14746560 | tf_op jit(solution)/shard_map/div | solution.py:75
  73.7 4.4 %fusion.27 = f32[6,960,320]{1,2,0:T(8,128)} fusion(bf16[320,6,128]{0,2,1:T(8,128)(2,1)S(1)} %bitcast.66, bf16[320,6,128]{2,0,1:T(8,128)(2,1)S(1)} %copy.96, bf16[320,6,128]{2,0,1:T(8,128)(2,1)S(1)} %copy-done.1, bf16[320,6,128]{2,0,1:T(8,128)(2,1)S(1)} %copy-done.2), kind=kOutput, calls=%fused_computation.27 | convolution fusion | flops 476282880 | bytes 9338880 | tf_op jit(solution)/shard_map/qhd,khd->hqk/dot_general | solution.py:76
  78.0 14.1 %fusion.18 = f32[960,6,128]{2,0,1:T(8,128)} fusion(bf16[320,6,128]{0,2,1:T(8,128)(2,1)S(1)} %bitcast.65, f32[6,320,960]{2,1,0:T(8,128)} %fusion.16, f32[6,960,320]{1,2,0:T(8,128)} %fusion.27), kind=kOutput, calls=%fused_computation.20 | convolution fusion | flops 481078080 | bytes 18186240 | tf_op jit(solution)/shard_map/hqk,qhd->khd/dot_general | solution.py:79
  92.1 3.3 %fusion.44 = (f32[320,6,128]{2,0,1:T(8,128)S(1)}, f32[320,6,128]{2,0,1:T(8,128)}, f32[320,6,128]{2,0,1:T(8,128)}) fusion(f32[960,6,128]{2,0,1:T(8,128)} %fusion.18), kind=kLoop, calls=%fused_computation.50 | loop fusion | bytes 5898240 | tf_op jit(solution)/shard_map/slice | solution.py:126
  95.4 1.6 copy.102
  97.0 1.5 copy.103
  98.5 3.0 %collective-permute-start.4 = (f32[320,768]{1,0:T(8,128)}, f32[320,768]{1,0:T(8,128)}, u32[]{:S(2)}, u32[]{:S(2)}) collective-permute-start(f32[320,768]{1,0:T(8,128)} %copy.103), channel_id=1, source_target_pairs={{1,0},{2,1},{3,2},{4,3},{5,4},{6,5},{7,6},{8,7},{9,8},{10,9},{11,1... | collective-permute-start | bytes 2949128 | tf_op jit(solution)/shard_map/ppermute | solution.py:22
  101.6 1.6 copy.101
  103.1 1.3 copy.104
  104.5 18.3 %collective-permute-done.4 = f32[320,768]{1,0:T(8,128)} collective-permute-done((f32[320,768]{1,0:T(8,128)}, f32[320,768]{1,0:T(8,128)}, u32[]{:S(2)}, u32[]{:S(2)}) %collective-permute-start.4) | collective-permute-done | bytes 983072 | tf_op jit(solution)/shard_map/ppermute | solution.py:22
  122.7 2.6 add.27
  125.3 4.8 %collective-permute-start.5 = (f32[320,768]{1,0:T(8,128)}, f32[320,768]{1,0:T(8,128)}, u32[]{:S(2)}, u32[]{:S(2)}) collective-permute-start(f32[320,768]{1,0:T(8,128)} %add.27), channel_id=1, source_target_pairs={{1,0},{2,1},{3,2},{4,3},{5,4},{6,5},{7,6},{8,7},{9,8},{10,9},{11,1... | collective-permute-start | bytes 2949128 | tf_op jit(solution)/shard_map/ppermute | solution.py:22
  130.5 18.5 %collective-permute-done.5 = f32[320,768]{1,0:T(8,128)} collective-permute-done((f32[320,768]{1,0:T(8,128)}, f32[320,768]{1,0:T(8,128)}, u32[]{:S(2)}, u32[]{:S(2)}) %collective-permute-start.5) | collective-permute-done | bytes 983072 | tf_op jit(solution)/shard_map/ppermute | solution.py:22
  149.0 1.6 copy.105
  151.6 62.3 %all_to_all.10 = f32[32,24,768]{2,1,0:T(8,128)S(1)} all-to-all(f32[32,24,768]{2,1,0:T(8,128)S(1)} %bitcast.61), channel_id=1, replica_groups=mesh['clip'=16,'tm'=32] {'tm'}, dimensions={0} | all-to-all | bytes 4718592 | tf_op jit(solution)/shard_map/all_to_all | solution.py:33
  214.1 45.9 %all_to_all.11 = f32[16,24,768]{2,1,0:T(8,128)S(1)} all-to-all(f32[16,24,768]{2,1,0:T(8,128)S(1)} %broadcast_in_dim.36), channel_id=1, replica_groups=mesh['clip'=16,'tm'=32] {'clip'}, dimensions={0} | all-to-all | bytes 2359296 | tf_op jit(solution)/shard_map/all_to_all | solution.py:39
  (31 shorter events, 8.5 us)
Async XLA Ops:
  0.6 150.1 %copy-start = (bf16[1,320,768]{2,1,0:T(8,128)(2,1)S(1)}, bf16[1,320,768]{2,1,0:T(8,128)(2,1)}, u32[]{:S(2)}) copy-start(bf16[1,320,768]{2,1,0:T(8,128)(2,1)} %param.9) | copy-start | bytes 1474564
  0.6 21.9 %collective-permute-start = (bf16[320,768]{1,0:T(8,128)(2,1)}, bf16[320,768]{1,0:T(8,128)(2,1)}, u32[]{:S(2)}, u32[]{:S(2)}) collective-permute-start(bf16[320,768]{1,0:T(8,128)(2,1)} %bitcast.73), channel_id=1, source_target_pairs={{0,1},{1,2},{2,3},{3,4},{4,5},{5,6},{6,7},{7,8},{8,9},{9,10},{10,1... | collective-permute-start | bytes 1474568 | tf_op jit(solution)/shard_map/ppermute | solution.py:22
  4.8 28.3 %collective-permute-start.2 = (bf16[320,768]{1,0:T(8,128)(2,1)}, bf16[320,768]{1,0:T(8,128)(2,1)}, u32[]{:S(2)}, u32[]{:S(2)}) collective-permute-start(bf16[320,768]{1,0:T(8,128)(2,1)} %bitcast.74), channel_id=1, source_target_pairs={{0,1},{1,2},{2,3},{3,4},{4,5},{5,6},{6,7},{7,8},{8,9},{9,10},{10,1... | collective-permute-start | bytes 1474568 | tf_op jit(solution)/shard_map/ppermute | solution.py:22
  22.6 25.9 %collective-permute-start.1 = (bf16[320,768]{1,0:T(8,128)(2,1)}, bf16[320,768]{1,0:T(8,128)(2,1)}, u32[]{:S(2)}, u32[]{:S(2)}) collective-permute-start(bf16[320,768]{1,0:T(8,128)(2,1)} %collective-permute-done), channel_id=1, source_target_pairs={{0,1},{1,2},{2,3},{3,4},{4,5},{5,6},{6,7},{7,8},{8,9},{9,10},{10,1... | collective-permute-start | bytes 1474568 | tf_op jit(solution)/shard_map/ppermute | solution.py:22
  33.1 21.1 %collective-permute-start.3 = (bf16[320,768]{1,0:T(8,128)(2,1)}, bf16[320,768]{1,0:T(8,128)(2,1)}, u32[]{:S(2)}, u32[]{:S(2)}) collective-permute-start(bf16[320,768]{1,0:T(8,128)(2,1)} %collective-permute-done.2), channel_id=1, source_target_pairs={{0,1},{1,2},{2,3},{3,4},{4,5},{5,6},{6,7},{7,8},{8,9},{9,10},{10,1... | collective-permute-start | bytes 1474568 | tf_op jit(solution)/shard_map/ppermute | solution.py:22
  62.1 11.5 %copy-start.1 = (bf16[320,6,128]{2,0,1:T(8,128)(2,1)S(1)}, bf16[320,6,128]{2,0,1:T(8,128)(2,1)}, u32[]{:S(2)}) copy-start(bf16[320,6,128]{2,0,1:T(8,128)(2,1)} %copy.95) | copy-start | bytes 1474564
  62.1 11.5 %copy-start.2 = (bf16[320,6,128]{2,0,1:T(8,128)(2,1)S(1)}, bf16[320,6,128]{2,0,1:T(8,128)(2,1)}, u32[]{:S(2)}) copy-start(bf16[320,6,128]{2,0,1:T(8,128)(2,1)} %copy.94) | copy-start | bytes 1474564
  98.5 24.2 %collective-permute-start.4 = (f32[320,768]{1,0:T(8,128)}, f32[320,768]{1,0:T(8,128)}, u32[]{:S(2)}, u32[]{:S(2)}) collective-permute-start(f32[320,768]{1,0:T(8,128)} %copy.103), channel_id=1, source_target_pairs={{1,0},{2,1},{3,2},{4,3},{5,4},{6,5},{7,6},{8,7},{9,8},{10,9},{11,1... | collective-permute-start | bytes 2949128 | tf_op jit(solution)/shard_map/ppermute | solution.py:22
  125.3 23.7 %collective-permute-start.5 = (f32[320,768]{1,0:T(8,128)}, f32[320,768]{1,0:T(8,128)}, u32[]{:S(2)}, u32[]{:S(2)}) collective-permute-start(f32[320,768]{1,0:T(8,128)} %add.27), channel_id=1, source_target_pairs={{1,0},{2,1},{3,2},{4,3},{5,4},{6,5},{7,6},{8,7},{9,8},{10,9},{11,1... | collective-permute-start | bytes 2949128 | tf_op jit(solution)/shard_map/ppermute | solution.py:22
  213.9 46.2 %copy-start.3 = (f32[24,768]{1,0:T(8,128)S(1)}, f32[24,768]{1,0:T(8,128)}, u32[]{:S(2)}) copy-start(f32[24,768]{1,0:T(8,128)} %param.15) | copy-start | bytes 221188
  213.9 46.2 %copy-start.4 = (f32[24,768]{1,0:T(8,128)S(1)}, f32[24,768]{1,0:T(8,128)}, u32[]{:S(2)}) copy-start(f32[24,768]{1,0:T(8,128)} %param.16) | copy-start | bytes 221188
  213.9 46.2 %copy-start.5 = (f32[24,768]{1,0:T(8,128)S(1)}, f32[24,768]{1,0:T(8,128)}, u32[]{:S(2)}) copy-start(f32[24,768]{1,0:T(8,128)} %param.17) | copy-start | bytes 221188
where the time goes:
time: 262 us; the launch traced here: 261 us
  blocking collectives  108 us (41%)
  waiting for transfers between devices  62.5 us (24%)
  local copies, waits for them, and re-layouts  28.1 us (11%)
  matrix products  24.9 us (10%)
  starting transfers between devices  19.8 us (8%)
  other arithmetic  15.2 us (6%)
    ppermute x6, waiting for transfers between devices, from_behind(): lax.ppermute(value, axis, [(source, source + steps) for source in range(l...  62.5 us
    all_to_all x1, blocking collectives, summed_on_arrival(): lax.all_to_all(cut_along(value, dim, length), axis, 0, 0, tiled=True)  62.3 us
    all_to_all x1, blocking collectives, copy_for_each(): lax.all_to_all(jnp.broadcast_to(value[None], (length, *value.shape)), axi...  45.9 us
    ppermute x6, starting transfers between devices, from_behind(): lax.ppermute(value, axis, [(source, source + steps) for source in range(l...  19.8 us
    dot_general x1, matrix products, window_grad(): jnp.einsum('hqk,qhd->khd', dscores, query_heads, preferred_element_type=j...  14.1 us
    div x1, other arithmetic, window_grad(): softmax = raised / jnp.sum(raised, axis=-1, keepdims=True)  11.5 us
    ppermute x5, local copies, waits for them, and re-layouts, from_behind(): lax.ppermute(value, axis, [(source, source + steps) for source in range(l...  6.89 us
    dot_general x1, matrix products, window_grad(): jnp.einsum('qhd,khd->hqk', query_heads, key_heads, preferred_element_type...  5.56 us
  transfers between devices with their start and end apart: 6, of which 5 were waited for; matrix products, arithmetic and copies ran while one was open for 7% of the time, Pallas kernels for 0%

commit v1 on v0

v1 whole, which is shorter than its diff:
```python
import functools
import math

import jax
import jax.numpy as jnp
from jax import lax
from jax.experimental import pallas as pl
from jax.experimental.pallas import tpu as pltpu
from jax.sharding import PartitionSpec as P

HEAD_DIM = 128
MESH = pl.DeviceIdType.MESH
NEG = -1e30

ZN = 8
YN = 4
CORES = 2

beta_one = 0.9
beta_two = 0.95
learn_rate = 0.001
adam_eps = 1e-08
decay_rate = 0.1
step_count = 10.0


def adamw(weight, moment_one, moment_two, gradient):
    new_one = beta_one * moment_one + (1.0 - beta_one) * gradient
    new_two = beta_two * moment_two + (1.0 - beta_two) * gradient * gradient
    corr_one = new_one / (1.0 - beta_one**step_count)
    corr_two = new_two / (1.0 - beta_two**step_count)
    new_weight = weight - learn_rate * (
        corr_one / (jnp.sqrt(corr_two) + adam_eps) + decay_rate * weight
    )
    return (new_weight, new_one, new_two)


def dot_nt(a, b):
    return lax.dot_general(a, b, (((1,), (1,)), ((), ())), preferred_element_type=jnp.float32)


def dot_nn(a, b):
    return lax.dot_general(a, b, (((1,), (0,)), ((), ())), preferred_element_type=jnp.float32)


def kernel(
    x_hbm, q_hbm, k_hbm, v_hbm, g_hbm, flags,
    grad_out,
    xcat, xt, qo, ko, vo, go, qn, gn, kp, vp,
    e_own, dp_own, own_st, own_st_in, nf_st, nf_st_in, kgn,
    gbuf, a_in, abuf, b_in, bbuf, c_in, cbuf, d_in, ebuf, e_in,
    sem_loc, sem_locx, win_s, win_r, x_s, x_r, os_s, os_r, nf_s, nf_r,
    a_s, a_r, b_s, b_r, c_s, c_r, d_s, d_r, e_s, e_r,
):
    heads, tok, _ = qo.shape
    pairs = heads // CORES
    tm_n = lax.axis_size("tm")
    clip_n = lax.axis_size("clip")
    quads = clip_n // CORES
    t = lax.axis_index("tm")
    c = lax.axis_index("clip")
    core = lax.rem(c, CORES)
    quad = c // CORES
    z = lax.rem(t, ZN)
    y = t // ZN
    has_prev = t > 0
    has_next = t < tm_n - 1
    nxt = jnp.minimum(t + 1, tm_n - 1)
    prv = jnp.maximum(t - 1, 0)
    sibling = c + 1 - 2 * core

    def cols(h):
        return pl.ds(pl.multiple_of(h * HEAD_DIM, HEAD_DIM), HEAD_DIM)

    def remote(src, dst, ssem, rsem, where):
        return pltpu.make_async_remote_copy(
            src_ref=src, dst_ref=dst, send_sem=ssem, recv_sem=rsem,
            device_id=where, device_id_type=MESH,
        )

    def local_copies(h):
        return [
            pltpu.make_async_copy(src.at[0, :, cols(h)], dst.at[h], sem_loc.at[i, h])
            for i, (src, dst) in enumerate(((q_hbm, qo), (k_hbm, ko), (v_hbm, vo), (g_hbm, go)))
        ]

    def ahead(h):
        return [
            remote(src.at[0, :, cols(h)], dst.at[h], win_s.at[i, h], win_r.at[i, h], {"tm": nxt})
            for i, (src, dst) in enumerate(((k_hbm, kp), (v_hbm, vp)))
        ]

    def behind(h):
        return [
            remote(src.at[0, :, cols(h)], dst.at[h], win_s.at[2 + i, h], win_r.at[2 + i, h], {"tm": prv})
            for i, (src, dst) in enumerate(((q_hbm, qn), (g_hbm, gn)))
        ]

    x_copy = remote(x_hbm.at[0], xcat.at[pl.ds(tok, tok)], x_s.at[0], x_r.at[0], {"tm": nxt})
    x_local = pltpu.make_async_copy(x_hbm.at[0], xcat.at[pl.ds(0, tok)], sem_locx.at[0])
    os_copy = remote(own_st, own_st_in, os_s.at[0], os_r.at[0], {"tm": prv})

    def nf_copy(h):
        return remote(nf_st.at[h], nf_st_in.at[h], nf_s.at[h], nf_r.at[h], {"tm": nxt})

    def a_copy(j):
        return remote(gbuf.at[j, 1 - core], a_in.at[j], a_s.at[j], a_r.at[j], {"clip": sibling})

    def b_copy(j, d):
        to = lax.rem(y + d, YN)
        return remote(abuf.at[j, to], b_in.at[j, d - 1], b_s.at[j, d - 1], b_r.at[j, d - 1],
                      {"tm": to * ZN + z})

    def c_copy(j, d):
        to = lax.rem(z + d, ZN)
        return remote(bbuf.at[j, to], c_in.at[j, d - 1], c_s.at[j, d - 1], c_r.at[j, d - 1],
                      {"tm": y * ZN + to})

    def d_copy(j, d):
        to = lax.rem(quad + d, quads)
        return remote(cbuf.at[j], d_in.at[j, d - 1], d_s.at[j, d - 1], d_r.at[j, d - 1],
                      {"clip": to * CORES + core})

    e_copy = remote(ebuf, e_in, e_s.at[0], e_r.at[0], {"clip": sibling})

    def each(lo, hi, fn):
        def step(i, carry):
            fn(i)
            return carry
        lax.fori_loop(lo, hi, step, 0)

    def start_local(h):
        for cp in local_copies(h):
            cp.start()
    each(0, heads, start_local)
    x_local.start()

    bar = pltpu.get_barrier_semaphore()
    def hello(where):
        pl.semaphore_signal(bar, inc=1, device_id=where, device_id_type=MESH)
    @pl.when(has_prev)
    def _():
        hello({"tm": prv})
    @pl.when(has_next)
    def _():
        hello({"tm": nxt})
    hello({"clip": sibling})
    each(1, YN, lambda d: hello({"tm": lax.rem(y + d, YN) * ZN + z}))
    each(1, ZN, lambda d: hello({"tm": y * ZN + lax.rem(z + d, ZN)}))
    each(1, quads, lambda d: hello({"clip": lax.rem(quad + d, quads) * CORES + core}))
    count = 1 + (YN - 1) + (ZN - 1) + (quads - 1)
    pl.semaphore_wait(bar, count + has_prev.astype(jnp.int32) + has_next.astype(jnp.int32))

    def send_window(h):
        @pl.when(has_next)
        def _():
            for cp in ahead(h):
                cp.start()
        @pl.when(has_prev)
        def _():
            for cp in behind(h):
                cp.start()

    @pl.when(has_next)
    def _():
        x_copy.start()
    send_window(0)
    send_window(1)

    @pl.when(jnp.logical_not(has_prev))
    def _():
        kp[...] = jnp.zeros_like(kp)
        vp[...] = jnp.zeros_like(vp)
        xcat[pl.ds(tok, tok), :] = jnp.zeros((tok, xcat.shape[1]), xcat.dtype)
        nf_st_in[...] = jnp.zeros_like(nf_st_in)
        nf_st_in[:, 0:1, :] = jnp.full((heads, 1, nf_st_in.shape[2]), NEG, jnp.float32)

    @pl.when(jnp.logical_not(has_next))
    def _():
        qn[...] = jnp.zeros_like(qn)
        gn[...] = jnp.zeros_like(gn)
        own_st_in[...] = jnp.ones_like(own_st_in)

    scaling = 1.0 / math.sqrt(HEAD_DIM)
    to_log2 = scaling * math.log2(math.e)

    def block(kk, vv, qq, gg):
        s = dot_nt(kk, qq) * to_log2
        m = jnp.max(s, axis=0, keepdims=True)
        e = jnp.exp2(s - m)
        l = jnp.sum(e, axis=0, keepdims=True)
        dp = dot_nt(vv, gg)
        d = jnp.sum(e * dp, axis=0, keepdims=True)
        return e, dp, m, l, d

    def put(ref, h, m, l, d):
        ref[h, 0:1, 0:tok] = m
        ref[h, 1:2, 0:tok] = l
        ref[h, 2:3, 0:tok] = d

    def get(ref, h):
        return ref[h, 0:1, 0:tok], ref[h, 1:2, 0:tok], ref[h, 2:3, 0:tok]

    own_st[...] = jnp.zeros_like(own_st)
    nf_st[...] = jnp.zeros_like(nf_st)

    def own_block(h):
        for cp in local_copies(h):
            cp.wait()
        e, dp, m, l, d = block(ko[h], vo[h], qo[h], go[h])
        e_own[h] = e
        dp_own[h] = dp
        put(own_st, h, m, l, d)
    each(0, heads, own_block)

    @pl.when(has_prev)
    def _():
        os_copy.start()
    @pl.when(has_next)
    def _():
        os_copy.wait_recv()

    fo = flags[0, t]
    fn = flags[0, nxt]
    near_ok = jnp.logical_and(fn == 0, has_next)
    far_ok = jnp.logical_and(jnp.logical_and(near_ok, fo == 0), has_prev)

    def total(ma, la, da, mb, lb, db):
        mt = jnp.maximum(ma, mb)
        fa = jnp.exp2(ma - mt)
        fb = jnp.exp2(mb - mt)
        inv = 1.0 / (fa * la + fb * lb)
        return fa, fb, inv, (fa * da + fb * db) * inv

    def near_far(h):
        @pl.when(h + 2 < heads)
        def _():
            send_window(h + 2)
        @pl.when(has_prev)
        def _():
            for cp in ahead(h):
                cp.wait_recv()
        @pl.when(has_next)
        def _():
            for cp in behind(h):
                cp.wait_recv()
        qq, gg = qn[h], gn[h]
        e1, dp1, m1, l1, d1 = block(ko[h], vo[h], qq, gg)
        e2, dp2, m2, l2, d2 = block(kp[h], vp[h], qq, gg)
        zero = jnp.zeros_like(m1)
        m1p = jnp.where(near_ok, m1, NEG)
        m2p = jnp.where(far_ok, m2, NEG)
        mb = jnp.maximum(m1p, m2p)
        f1 = jnp.where(near_ok, jnp.exp2(m1p - mb), zero)
        f2 = jnp.where(far_ok, jnp.exp2(m2p - mb), zero)
        lb = f1 * l1 + f2 * l2
        db = f1 * d1 + f2 * d2
        put(nf_st, h, mb, lb, db)
        @pl.when(has_next)
        def _():
            nf_copy(h).start()
        ma, la, da = get(own_st_in, h)
        _, fb, inv, delta = total(ma, la, da, mb, lb, db)
        w = fb * inv * scaling
        ds1 = ((e1 * (f1 * w)) * (dp1 - delta)).astype(jnp.bfloat16)
        ds2 = ((e2 * (f2 * w)) * (dp2 - delta)).astype(jnp.bfloat16)
        kgn[h, 0:tok] = dot_nn(ds1, qq)
        kgn[h, tok : 2 * tok] = dot_nn(ds2, qq)

    def finish(h):
        @pl.when(has_prev)
        def _():
            nf_copy(h).wait_recv()
        ma, la, da = get(own_st, h)
        mb, lb, db = get(nf_st_in, h)
        fa, _, inv, delta = total(ma, la, da, mb, lb, db)
        ds = ((e_own[h] * (fa * inv * scaling)) * (dp_own[h] - delta)).astype(jnp.bfloat16)
        kgn[h, 0:tok] = kgn[h, 0:tok] + dot_nn(ds, qo[h])
        grad = dot_nn(xt[...], kgn[h].astype(jnp.bfloat16))
        gbuf[h // CORES, lax.rem(h, CORES)] = grad.astype(jnp.bfloat16).reshape(gbuf.shape[2:])

    f32 = jnp.float32

    def a_finish(j):
        a_copy(j).wait_recv()
        abuf[j] = (gbuf[j, core].astype(f32) + a_in[j].astype(f32)).astype(jnp.bfloat16)
        each(1, YN, lambda d: b_copy(j, d).start())

    def b_finish(j):
        each(1, YN, lambda d: b_copy(j, d).wait_recv())
        acc = abuf[j, y].astype(f32)
        for d in range(YN - 1):
            acc = acc + b_in[j, d].astype(f32)
        bbuf[j] = acc.reshape(bbuf.shape[1:])
        each(1, ZN, lambda d: c_copy(j, d).start())

    def c_finish(j):
        each(1, ZN, lambda d: c_copy(j, d).wait_recv())
        acc = bbuf[j, z]
        for d in range(ZN - 1):
            acc = acc + c_in[j, d]
        cbuf[j] = acc
        each(1, quads, lambda d: d_copy(j, d).start())

    def d_finish(j):
        each(1, quads, lambda d: d_copy(j, d).wait_recv())
        acc = cbuf[j]
        for d in range(quads - 1):
            acc = acc + d_in[j, d]
        ebuf[j] = acc

    def main(h, carry):
        @pl.when(h < heads)
        def _():
            near_far(h)
        @pl.when(h == 0)
        def _():
            x_local.wait()
            @pl.when(has_prev)
            def _():
                x_copy.wait_recv()
            xt[...] = xcat[...].T
        @pl.when(h > 0)
        def _():
            finish(h - 1)
        j = h // 2 - 1
        @pl.when(jnp.logical_and(lax.rem(h, 2) == 0, h > 0))
        def _():
            a_copy(j).start()
        @pl.when(jnp.logical_and(lax.rem(h, 2) == 0, h > 2))
        def _():
            b_finish(j - 1)
        @pl.when(jnp.logical_and(lax.rem(h, 2) == 1, h > 2))
        def _():
            a_finish(j)
        @pl.when(jnp.logical_and(lax.rem(h, 2) == 1, h > 4))
        def _():
            c_finish(j - 1)
        return carry
    lax.fori_loop(0, heads + 1, main, 0)

    last = pairs - 1
    a_finish(last)
    c_finish(last - 1)
    b_finish(last)
    each(0, last, d_finish)
    c_finish(last)
    d_finish(last)
    e_copy.start()
    for j in range(pairs):
        grad_out[:, cols(j * CORES + core)] = ebuf[j]
    e_copy.wait_recv()
    for j in range(pairs):
        grad_out[:, cols(j * CORES + 1 - core)] = e_in[j]

    @pl.when(has_next)
    def _():
        x_copy.wait_send()
        def sent(h):
            for cp in ahead(h):
                cp.wait_send()
            nf_copy(h).wait_send()
        each(0, heads, sent)
    @pl.when(has_prev)
    def _():
        os_copy.wait_send()
        def sent(h):
            for cp in behind(h):
                cp.wait_send()
        each(0, heads, sent)
    def sent_pair(j):
        a_copy(j).wait_send()
        each(1, YN, lambda d: b_copy(j, d).wait_send())
        each(1, ZN, lambda d: c_copy(j, d).wait_send())
        each(1, quads, lambda d: d_copy(j, d).wait_send())
    each(0, pairs, sent_pair)
    e_copy.wait_send()


def body(
    inputs, query_states, key_states, value_states, out_grad, first_flags,
    weight, moment_one, moment_two,
):
    _, tok, width = query_states.shape
    feats = inputs.shape[2]
    heads = width // HEAD_DIM
    pairs = heads // CORES
    rows = weight.shape[0]
    quads = lax.axis_size("clip") // CORES
    per_y = rows * ZN
    bf, f32 = jnp.bfloat16, jnp.float32
    V = pltpu.VMEM
    lanes = (tok + 127) // 128 * 128
    dma = pltpu.SemaphoreType.DMA
    scratch = (
        [V((2 * tok, feats), bf), V((feats, 2 * tok), bf)]
        + [V((heads, tok, HEAD_DIM), bf)] * 8
        + [V((heads, tok, tok), f32)] * 2
        + [V((heads, 8, lanes), f32)] * 4
        + [V((heads, 2 * tok, HEAD_DIM), f32)]
        + [
            V((pairs, CORES, YN, per_y, HEAD_DIM), bf),
            V((pairs, YN, per_y, HEAD_DIM), bf),
            V((pairs, YN, per_y, HEAD_DIM), bf),
            V((pairs, YN - 1, per_y, HEAD_DIM), bf),
            V((pairs, ZN, rows, HEAD_DIM), f32),
            V((pairs, ZN - 1, rows, HEAD_DIM), f32),
            V((pairs, rows, HEAD_DIM), f32),
            V((pairs, quads - 1, rows, HEAD_DIM), f32),
            V((pairs, rows, HEAD_DIM), f32),
            V((pairs, rows, HEAD_DIM), f32),
        ]
        + [dma((4, heads)), dma((1,))]
        + [dma((4, heads))] * 2
        + [dma((1,))] * 2
        + [dma((1,))] * 2
        + [dma((heads,))] * 2
        + [dma((pairs,))] * 2
        + [dma((pairs, YN - 1))] * 2
        + [dma((pairs, ZN - 1))] * 2
        + [dma((pairs, quads - 1))] * 2
        + [dma((1,))] * 2
    )
    gradient = pl.pallas_call(
        kernel,
        out_shape=jax.ShapeDtypeStruct((rows, width), f32),
        in_specs=[pl.BlockSpec(memory_space=pl.ANY)] * 5 + [pl.BlockSpec(memory_space=pltpu.SMEM)],
        out_specs=pl.BlockSpec(memory_space=pltpu.VMEM),
        scratch_shapes=scratch,
        compiler_params=pltpu.CompilerParams(
            collective_id=0, has_side_effects=True, vmem_limit_bytes=48 * 1024 * 1024
        ),
        cost_estimate=pl.CostEstimate(flops=2_000_000_000, bytes_accessed=3_000_000, transcendentals=2_000_000),
    )(inputs, query_states, key_states, value_states, out_grad, first_flags)
    return adamw(weight, moment_one, moment_two, gradient)


def solution(mesh):
    in_specs = (
        P("clip", "tm", None),
        P("clip", "tm", None),
        P("clip", "tm", None),
        P("clip", "tm", None),
        P("clip", "tm", None),
        P("clip", None),
        P("tm", None),
        P("tm", None),
        P("tm", None),
    )
    out_specs = (P("tm", None), P("tm", None), P("tm", None))
    return jax.shard_map(body, mesh=mesh, in_specs=in_specs, out_specs=out_specs, check_vma=False)
```

time: 262 us -> 92.8 us (0.35)
  the two profiles are of different devices: /device:TPU:9 before, /device:TPU:57 now
where the time goes in v1:
time: 92.8 us; the launch traced here: 92.4 us
  Pallas kernels  85.3 us (92%)
  local copies, waits for them, and re-layouts  5.81 us (6%)
    pallas_call x1, Pallas kernels, body(): pl.pallas_call(kernel, out_shape=jax.ShapeDtypeStruct((rows, width), f32)...  85.3 us
    unnamed x18, local copies, waits for them, and re-layouts  5.81 us

profile of v1, /device:TPU:57, one launch (start us, length us, event | category | flops | bytes accessed | tf_op | source)
XLA Modules:
  0.0 92.4 jit_solution(2977852068014570658)
XLA Ops:
  0.6 0.0 copy-start
  0.6 1.0 %copy-done = bf16[1,320,768]{2,1,0:T(8,128)(2,1)S(1)} copy-done((bf16[1,320,768]{2,1,0:T(8,128)(2,1)S(1)}, bf16[1,320,768]{2,1,0:T(8,128)(2,1)}, u32[]{:S(2)}) %copy-start) | copy-done | bytes 491544
  1.7 0.0 copy-start.1
  1.7 1.0 %copy-done.1 = bf16[1,320,768]{2,1,0:T(8,128)(2,1)S(1)} copy-done((bf16[1,320,768]{2,1,0:T(8,128)(2,1)S(1)}, bf16[1,320,768]{2,1,0:T(8,128)(2,1)}, u32[]{:S(2)}) %copy-start.1) | copy-done | bytes 491544
  2.7 0.0 copy-start.2
  2.7 1.0 %copy-done.2 = bf16[1,320,768]{2,1,0:T(8,128)(2,1)S(1)} copy-done((bf16[1,320,768]{2,1,0:T(8,128)(2,1)S(1)}, bf16[1,320,768]{2,1,0:T(8,128)(2,1)}, u32[]{:S(2)}) %copy-start.2) | copy-done | bytes 491544
  3.7 0.0 copy-start.3
  3.7 1.0 %copy-done.3 = bf16[1,320,768]{2,1,0:T(8,128)(2,1)S(1)} copy-done((bf16[1,320,768]{2,1,0:T(8,128)(2,1)S(1)}, bf16[1,320,768]{2,1,0:T(8,128)(2,1)}, u32[]{:S(2)}) %copy-start.3) | copy-done | bytes 491544
  4.8 0.0 copy-start.4
  4.8 1.0 %copy-done.4 = bf16[1,320,768]{2,1,0:T(8,128)(2,1)S(1)} copy-done((bf16[1,320,768]{2,1,0:T(8,128)(2,1)S(1)}, bf16[1,320,768]{2,1,0:T(8,128)(2,1)}, u32[]{:S(2)}) %copy-start.4) | copy-done | bytes 491544
  5.8 0.0 copy-start.5
  5.8 0.7 copy-done.5
  6.4 0.0 copy-start.6
  6.4 0.0 copy-start.7
  6.4 0.0 copy-start.8
  6.4 85.3 %shard_map.112 = f32[24,768]{1,0:T(8,128)S(1)} custom-call(bf16[1,320,768]{2,1,0:T(8,128)(2,1)S(1)} %copy-done, bf16[1,320,768]{2,1,0:T(8,128)(2,1)S(1)} %copy-done.1, bf16[1,320,768]{2,1,0:T(8,128)(2,1)S(1)} %copy-done.2, bf16[1,320,768]{2,1,0:T(8,128)(2,1)S(1)} %copy-done.3, bf16[1,320,768]{2,1,0:T(8,128)(2,1)S(1)} %copy-done.4, s32[1,32]{1,0:T(1,128)S(1)} %copy-done.5), custom_call_target="tpu_custom_call" | custom-call | flops 2000000000 | bytes 3000000 | tf_op jit(solution)/shard_map/pallas_call | solution.py:424
  91.7 0.0 copy-done.6
  91.7 0.0 copy-done.7
  91.7 0.0 copy-done.8
  91.7 0.7 multiply_subtract_fusion
Async XLA Ops:
  0.6 1.0 %copy-start = (bf16[1,320,768]{2,1,0:T(8,128)(2,1)S(1)}, bf16[1,320,768]{2,1,0:T(8,128)(2,1)}, u32[]{:S(2)}) copy-start(bf16[1,320,768]{2,1,0:T(8,128)(2,1)} %x_hbm.1) | copy-start | bytes 1474564
  1.7 1.0 %copy-start.1 = (bf16[1,320,768]{2,1,0:T(8,128)(2,1)S(1)}, bf16[1,320,768]{2,1,0:T(8,128)(2,1)}, u32[]{:S(2)}) copy-start(bf16[1,320,768]{2,1,0:T(8,128)(2,1)} %q_hbm.1) | copy-start | bytes 1474564
  2.7 1.0 %copy-start.2 = (bf16[1,320,768]{2,1,0:T(8,128)(2,1)S(1)}, bf16[1,320,768]{2,1,0:T(8,128)(2,1)}, u32[]{:S(2)}) copy-start(bf16[1,320,768]{2,1,0:T(8,128)(2,1)} %k_hbm.1) | copy-start | bytes 1474564
  3.7 1.0 %copy-start.3 = (bf16[1,320,768]{2,1,0:T(8,128)(2,1)S(1)}, bf16[1,320,768]{2,1,0:T(8,128)(2,1)}, u32[]{:S(2)}) copy-start(bf16[1,320,768]{2,1,0:T(8,128)(2,1)} %v_hbm.1) | copy-start | bytes 1474564
  4.8 1.0 %copy-start.4 = (bf16[1,320,768]{2,1,0:T(8,128)(2,1)S(1)}, bf16[1,320,768]{2,1,0:T(8,128)(2,1)}, u32[]{:S(2)}) copy-start(bf16[1,320,768]{2,1,0:T(8,128)(2,1)} %g_hbm.1) | copy-start | bytes 1474564
  5.8 0.7 copy-start.5
  6.4 85.3 %copy-start.6 = (f32[24,768]{1,0:T(8,128)S(1)}, f32[24,768]{1,0:T(8,128)}, u32[]{:S(2)}) copy-start(f32[24,768]{1,0:T(8,128)} %param.15) | copy-start | bytes 221188
  6.4 85.3 %copy-start.7 = (f32[24,768]{1,0:T(8,128)S(1)}, f32[24,768]{1,0:T(8,128)}, u32[]{:S(2)}) copy-start(f32[24,768]{1,0:T(8,128)} %param.16) | copy-start | bytes 221188
  6.4 85.3 %copy-start.8 = (f32[24,768]{1,0:T(8,128)S(1)}, f32[24,768]{1,0:T(8,128)}, u32[]{:S(2)}) copy-start(f32[24,768]{1,0:T(8,128)} %param.17) | copy-start | bytes 221188

commit v2 on v1

v2 whole, which is shorter than its diff:
```python
import functools
import math

import jax
import jax.numpy as jnp
from jax import lax
from jax.experimental import pallas as pl
from jax.experimental.pallas import tpu as pltpu
from jax.sharding import PartitionSpec as P

HEAD_DIM = 128
MESH = pl.DeviceIdType.MESH
NEG = -1e30
VMEM_BYTES = 66_700_000

ZN = 8
YN = 4
YH = 2
CORES = 2
UNITS = ((0, 2), (2, 4), (4, 5), (5, 6))

beta_one = 0.9
beta_two = 0.95
learn_rate = 0.001
adam_eps = 1e-08
decay_rate = 0.1
step_count = 10.0


def adamw(weight, moment_one, moment_two, gradient):
    new_one = beta_one * moment_one + (1.0 - beta_one) * gradient
    new_two = beta_two * moment_two + (1.0 - beta_two) * gradient * gradient
    corr_one = new_one / (1.0 - beta_one**step_count)
    corr_two = new_two / (1.0 - beta_two**step_count)
    new_weight = weight - learn_rate * (
        corr_one / (jnp.sqrt(corr_two) + adam_eps) + decay_rate * weight
    )
    return (new_weight, new_one, new_two)


def dot_nt(a, b):
    return lax.dot_general(a, b, (((1,), (1,)), ((), ())), preferred_element_type=jnp.float32)


def dot_nn(a, b):
    return lax.dot_general(a, b, (((1,), (0,)), ((), ())), preferred_element_type=jnp.float32)


def kernel(
    x_hbm, q_hbm, k_hbm, v_hbm, g_hbm, flags_hbm,
    grad_out,
    flags, xcat, xt, qo, go, qn, gn, kc, vc,
    e_own, dp_own, own_st, own_st_in, nf_st, nf_st_in, kgn, ret, ret_in,
    *rest,
):
    nu = len(UNITS)
    gbuf, a_in, abuf, b_in, bbuf, c_in, cbuf, y_in, d_in = [rest[i * nu : (i + 1) * nu] for i in range(9)]
    (sem_loc, sem_locx, sem_f, win_s, win_r, x_s, x_r, os_s, os_r, nf_s, nf_r,
     ret_s, ret_r, a_s, a_r, b_s, b_r, c_s, c_r, y_s, y_r, d_s, d_r) = rest[9 * nu :]
    heads, tok, _ = qo.shape
    half = ZN // CORES
    rows = grad_out.shape[0]
    part = half * rows
    f32, bf = jnp.float32, jnp.bfloat16
    tm_n = lax.axis_size("tm")
    xn = lax.axis_size("clip") // (CORES * YH)
    ys = YN * YH
    t = lax.axis_index("tm")
    c = lax.axis_index("clip")
    core = lax.rem(c, CORES)
    x = c // (CORES * YH)
    z = lax.rem(t, ZN)
    y = lax.rem(c // CORES, YH) * YN + t // ZN
    y_lo = t // ZN
    holder = z // half == core
    final = jnp.logical_and(holder, x == y_lo)
    has_prev = t > 0
    has_next = t < tm_n - 1
    nxt = jnp.minimum(t + 1, tm_n - 1)
    prv = jnp.maximum(t - 1, 0)
    sibling = c + 1 - 2 * core

    def cols(h):
        return pl.ds(pl.multiple_of(h * HEAD_DIM, HEAD_DIM), HEAD_DIM)

    cut = tok // 2
    own_rows = pl.ds(0, tok)
    prev_rows = pl.ds(tok, tok)

    def remote(src, dst, ssem, rsem, where):
        return pltpu.make_async_remote_copy(
            src_ref=src, dst_ref=dst, send_sem=ssem, recv_sem=rsem,
            device_id=where, device_id_type=MESH,
        )

    def local_copies(h):
        places = (
            (q_hbm, qo.at[h]), (k_hbm, kc.at[h, own_rows]),
            (v_hbm, vc.at[h, own_rows]), (g_hbm, go.at[h]),
        )
        return [
            pltpu.make_async_copy(src.at[0, :, cols(h)], dst, sem_loc.at[i, h])
            for i, (src, dst) in enumerate(places)
        ]

    def ahead(h):
        return [
            remote(src.at[0, :, cols(h)], dst.at[h, prev_rows], win_s.at[i, h], win_r.at[i, h], {"tm": nxt})
            for i, (src, dst) in enumerate(((k_hbm, kc), (v_hbm, vc)))
        ]

    def behind(h):
        return [
            remote(src.at[0, :, cols(h)], dst.at[h], win_s.at[2 + i, h], win_r.at[2 + i, h], {"tm": prv})
            for i, (src, dst) in enumerate(((q_hbm, qn), (g_hbm, gn)))
        ]

    x_copy = remote(x_hbm.at[0, pl.ds(0, cut)], xcat.at[pl.ds(tok, cut)], x_s.at[0], x_r.at[0], {"tm": nxt})
    x_local = pltpu.make_async_copy(x_hbm.at[0], xcat.at[own_rows], sem_locx.at[0])
    f_local = pltpu.make_async_copy(flags_hbm, flags, sem_f.at[0])
    os_copy = remote(own_st, own_st_in, os_s.at[0], os_r.at[0], {"tm": prv})

    def nf_copy(h):
        return remote(nf_st.at[h], nf_st_in.at[h], nf_s.at[h], nf_r.at[h], {"tm": nxt})

    def ret_copy(h):
        return remote(ret.at[h], ret_in.at[h], ret_s.at[h], ret_r.at[h], {"tm": prv})

    def at_y(to):
        return {"clip": (x * YH + to // YN) * CORES + core, "tm": lax.rem(to, YN) * ZN + z}

    def at_z(to):
        return {"tm": y_lo * ZN + to}

    def at_x(d, to_core):
        return {"clip": lax.rem(x + d, xn) * (YH * CORES) + lax.rem(c, YH * CORES) - core + to_core}

    def a_copy(u):
        return remote(gbuf[u].at[1 - core], a_in[u], a_s.at[u], a_r.at[u], {"clip": sibling})

    def b_copy(u, d):
        return remote(abuf[u].at[lax.rem(x + d, xn)], b_in[u].at[d - 1], b_s.at[u, d - 1], b_r.at[u, d - 1], at_x(d, core))

    def c_copy(u, i):
        to = core * half + i
        slot = lax.rem(to - z + ZN - 1, ZN)
        return remote(bbuf[u].at[i], c_in[u].at[slot], c_s.at[u, i], c_r.at[u, slot], at_z(to))

    def c_arrival(u, slot):
        return remote(bbuf[u].at[0], c_in[u].at[slot], c_s.at[u, 0], c_r.at[u, slot], at_z(lax.rem(z + 1, ZN)))

    def y_copy(u, k):
        to = x + k * YN
        slot = lax.rem(to - y + 2 * ys - 1, ys)
        return remote(cbuf[u], y_in[u].at[slot], y_s.at[u, k], y_r.at[u, slot], at_y(to))

    def y_arrival(u, slot):
        return remote(cbuf[u], y_in[u].at[slot], y_s.at[u, 0], y_r.at[u, slot], at_y(lax.rem(y + 1, ys)))

    def d_copy(u, d, to_core):
        return remote(d_in[u], d_in[u], d_s.at[u, d, to_core], d_r.at[u], at_x(d, to_core))

    def d_near(u):
        return remote(d_in[u], d_in[u], d_s.at[u, 0, 0], d_r.at[u], {"clip": sibling})

    def each(lo, hi, fn):
        def step(i, carry):
            fn(i)
            return carry
        lax.fori_loop(lo, hi, step, 0)

    def start_local(h):
        for cp in local_copies(h):
            cp.start()
    each(0, heads, start_local)
    x_local.start()
    f_local.start()

    bar = pltpu.get_barrier_semaphore()
    def hello(where):
        pl.semaphore_signal(bar, inc=1, device_id=where, device_id_type=MESH)
    @pl.when(has_prev)
    def _():
        hello({"tm": prv})
    @pl.when(has_next)
    def _():
        hello({"tm": nxt})
    hello({"clip": sibling})
    each(1, ys, lambda d: hello(at_y(lax.rem(y + d, ys))))
    each(1, ZN, lambda d: hello(at_z(lax.rem(z + d, ZN))))
    for k in range(CORES):
        each(1, xn, lambda d: hello(at_x(d, k)))
    count = 1 + (ys - 1) + (ZN - 1) + CORES * (xn - 1)
    pl.semaphore_wait(bar, count + has_prev.astype(jnp.int32) + has_next.astype(jnp.int32))

    def send_window(h):
        @pl.when(has_next)
        def _():
            for cp in ahead(h):
                cp.start()
        @pl.when(has_prev)
        def _():
            for cp in behind(h):
                cp.start()

    send_window(0)
    @pl.when(has_next)
    def _():
        x_copy.start()
    send_window(1)

    @pl.when(jnp.logical_not(has_prev))
    def _():
        kc[:, tok : 2 * tok, :] = jnp.zeros((heads, tok, HEAD_DIM), bf)
        vc[:, tok : 2 * tok, :] = jnp.zeros((heads, tok, HEAD_DIM), bf)
        xcat[tok : tok + cut, :] = jnp.zeros((cut, xcat.shape[1]), bf)
        nf_st_in[...] = jnp.zeros_like(nf_st_in)
        nf_st_in[:, 0:1, :] = jnp.full((heads, 1, nf_st_in.shape[2]), NEG, f32)

    @pl.when(jnp.logical_not(has_next))
    def _():
        qn[...] = jnp.zeros_like(qn)
        gn[...] = jnp.zeros_like(gn)
        ret_in[...] = jnp.zeros_like(ret_in)
        own_st_in[...] = jnp.ones_like(own_st_in)

    scaling = 1.0 / math.sqrt(HEAD_DIM)
    to_log2 = scaling * math.log2(math.e)

    def stats(s, dp):
        m = jnp.max(s, axis=0, keepdims=True) * to_log2
        e = jnp.exp2(s * to_log2 - m)
        return e, m, jnp.sum(e, axis=0, keepdims=True), jnp.sum(e * dp, axis=0, keepdims=True)

    def put(ref, h, m, l, d):
        ref[h, 0:1, 0:tok] = m
        ref[h, 1:2, 0:tok] = l
        ref[h, 2:3, 0:tok] = d

    def get(ref, h):
        return ref[h, 0:1, 0:tok], ref[h, 1:2, 0:tok], ref[h, 2:3, 0:tok]

    own_st[...] = jnp.zeros_like(own_st)
    nf_st[...] = jnp.zeros_like(nf_st)

    def own_blocks(i):
        pair = (i * 2, i * 2 + 1)
        for h in pair:
            for cp in local_copies(h):
                cp.wait()
        for h in pair:
            s = dot_nt(kc[h, own_rows], qo[h])
            dp = dot_nt(vc[h, own_rows], go[h])
            e, m, l, d = stats(s, dp)
            e_own[h] = e
            dp_own[h] = dp
            put(own_st, h, m, l, d)
    each(0, heads // 2, own_blocks)

    @pl.when(has_prev)
    def _():
        os_copy.start()
    @pl.when(has_next)
    def _():
        os_copy.wait_recv()

    f_local.wait()
    fo = flags[0, t]
    fn = flags[0, nxt]
    near_ok = jnp.logical_and(fn == 0, has_next)
    far_ok = jnp.logical_and(jnp.logical_and(near_ok, fo == 0), has_prev)

    def total(ma, la, da, mb, lb, db):
        mt = jnp.maximum(ma, mb)
        fa = jnp.exp2(ma - mt)
        fb = jnp.exp2(mb - mt)
        inv = 1.0 / (fa * la + fb * lb)
        return fa, fb, inv, (fa * da + fb * db) * inv

    def near_far(h):
        @pl.when(h + 2 < heads)
        def _():
            send_window(h + 2)
        @pl.when(has_prev)
        def _():
            for cp in ahead(h):
                cp.wait_recv()
        @pl.when(has_next)
        def _():
            for cp in behind(h):
                cp.wait_recv()
        qq, gg = qn[h], gn[h]
        s = dot_nt(kc[h], qq)
        dp = dot_nt(vc[h], gg)
        e1, m1, l1, d1 = stats(s[:tok], dp[:tok])
        e2, m2, l2, d2 = stats(s[tok:], dp[tok:])
        zero = jnp.zeros_like(m1)
        m1p = jnp.where(near_ok, m1, NEG)
        m2p = jnp.where(far_ok, m2, NEG)
        mb = jnp.maximum(m1p, m2p)
        f1 = jnp.where(near_ok, jnp.exp2(m1p - mb), zero)
        f2 = jnp.where(far_ok, jnp.exp2(m2p - mb), zero)
        lb = f1 * l1 + f2 * l2
        db = f1 * d1 + f2 * d2
        put(nf_st, h, mb, lb, db)
        @pl.when(has_next)
        def _():
            nf_copy(h).start()
        ma, la, da = get(own_st_in, h)
        _, fb, inv, delta = total(ma, la, da, mb, lb, db)
        w = fb * inv * scaling
        ds1 = ((e1 * (f1 * w)) * (dp[:tok] - delta)).astype(bf)
        ds2 = ((e2 * (f2 * w)) * (dp[tok:] - delta)).astype(bf)
        kg = dot_nn(jnp.concatenate([ds1, ds2], axis=0), qq)
        kgn[h] = kg[: tok + cut]
        ret[h] = kg[tok + cut :].astype(bf)
        @pl.when(has_prev)
        def _():
            ret_copy(h).start()

    def finish(h):
        @pl.when(has_prev)
        def _():
            nf_copy(h).wait_recv()
        @pl.when(has_next)
        def _():
            ret_copy(h).wait_recv()
        ma, la, da = get(own_st, h)
        mb, lb, db = get(nf_st_in, h)
        fa, _, inv, delta = total(ma, la, da, mb, lb, db)
        ds = ((e_own[h] * (fa * inv * scaling)) * (dp_own[h] - delta)).astype(bf)
        own = dot_nn(ds, qo[h])
        back = ret_in[h].astype(f32)
        kg = jnp.concatenate(
            [kgn[h, 0:cut] + own[:cut], kgn[h, cut:tok] + own[cut:] + back, kgn[h, tok : tok + cut]], axis=0
        ).astype(bf)
        grad = dot_nn(xt[...], kg).astype(bf)
        for u, (lo, hi) in enumerate(UNITS):
            @pl.when(jnp.logical_and(h >= lo, h < hi))
            def _():
                for yy in range(YN):
                    for k in range(CORES):
                        at = (yy * CORES + k) * part
                        gbuf[u][k, yy, :, cols(h - lo)] = grad[at : at + part]

    def a_finish(u):
        a_copy(u).wait_recv()
        for yy in range(YN):
            abuf[u][yy] = (gbuf[u][core, yy].astype(f32) + a_in[u][yy].astype(f32)).astype(bf)
        each(1, xn, lambda d: b_copy(u, d).start())

    def b_finish(u):
        each(1, xn, lambda d: b_copy(u, d).wait_recv())
        acc = abuf[u][x].astype(f32)
        for d in range(xn - 1):
            acc = acc + b_in[u][d].astype(f32)
        bbuf[u][...] = acc.reshape(bbuf[u].shape)
        def send(i):
            @pl.when(core * half + i != z)
            def _():
                c_copy(u, i).start()
        each(0, half, send)

    def c_finish(u):
        @pl.when(holder)
        def _():
            each(0, ZN - 1, lambda i: c_arrival(u, i).wait_recv())
            acc = bbuf[u][lax.rem(z, half)]
            for i in range(ZN - 1):
                acc = acc + c_in[u][i]
            cbuf[u][...] = acc
            def send(k):
                @pl.when(x + k * YN != y)
                def _():
                    y_copy(u, k).start()
            each(0, YH, send)

    def y_finish(u):
        @pl.when(final)
        def _():
            each(0, ys - 1, lambda i: y_arrival(u, i).wait_recv())
            acc = cbuf[u][...]
            for i in range(ys - 1):
                acc = acc + y_in[u][i]
            d_in[u][...] = acc
            d_near(u).start()
            for k in range(CORES):
                each(1, xn, lambda d: d_copy(u, d, k).start())

    def d_finish(u):
        @pl.when(jnp.logical_not(final))
        def _():
            d_near(u).wait_recv()
        lo, hi = UNITS[u]
        grad_out[:, lo * HEAD_DIM : hi * HEAD_DIM] = d_in[u][...]

    def main(h, carry):
        @pl.when(h < heads)
        def _():
            near_far(h)
        @pl.when(h == 0)
        def _():
            x_local.wait()
            @pl.when(has_prev)
            def _():
                x_copy.wait_recv()
            xt[...] = xcat[...].T
        @pl.when(h == 6)
        def _():
            a_finish(2)
        @pl.when(h > 0)
        def _():
            finish(h - 1)
        @pl.when(h == 2)
        def _():
            a_copy(0).start()
        @pl.when(h == 3)
        def _():
            a_finish(0)
        @pl.when(h == 4)
        def _():
            a_copy(1).start()
        @pl.when(h == 5)
        def _():
            a_copy(2).start()
            a_finish(1)
            b_finish(0)
        return carry
    lax.fori_loop(0, heads + 1, main, 0)

    a_copy(3).start()
    b_finish(1)
    c_finish(0)
    a_finish(3)
    b_finish(2)
    y_finish(0)
    c_finish(1)
    b_finish(3)
    c_finish(2)
    y_finish(1)
    c_finish(3)
    y_finish(2)
    d_finish(0)
    d_finish(1)
    y_finish(3)
    d_finish(2)
    d_finish(3)

    @pl.when(has_next)
    def _():
        x_copy.wait_send()
        def sent(h):
            for cp in ahead(h):
                cp.wait_send()
            nf_copy(h).wait_send()
        each(0, heads, sent)
    @pl.when(has_prev)
    def _():
        os_copy.wait_send()
        def sent(h):
            for cp in behind(h):
                cp.wait_send()
            ret_copy(h).wait_send()
        each(0, heads, sent)
    for u in range(nu):
        a_copy(u).wait_send()
        each(1, xn, lambda d: b_copy(u, d).wait_send())
        def left(i):
            @pl.when(core * half + i != z)
            def _():
                c_copy(u, i).wait_send()
        each(0, half, left)
        @pl.when(holder)
        def _():
            def left_y(k):
                @pl.when(x + k * YN != y)
                def _():
                    y_copy(u, k).wait_send()
            each(0, YH, left_y)
        @pl.when(final)
        def _():
            d_near(u).wait_send()
            for k in range(CORES):
                each(1, xn, lambda d: d_copy(u, d, k).wait_send())


def body(
    inputs, query_states, key_states, value_states, out_grad, first_flags,
    weight, moment_one, moment_two,
):
    _, tok, width = query_states.shape
    feats = inputs.shape[2]
    heads = width // HEAD_DIM
    rows = weight.shape[0]
    xn = lax.axis_size("clip") // (CORES * YH)
    ys = YN * YH
    half = ZN // CORES
    part = half * rows
    wide = [(hi - lo) * HEAD_DIM for lo, hi in UNITS]
    nu = len(UNITS)
    bf, f32 = jnp.bfloat16, jnp.float32
    V = pltpu.VMEM
    lanes = (tok + 127) // 128 * 128
    dma = pltpu.SemaphoreType.DMA
    scratch = (
        [pltpu.SMEM(first_flags.shape, jnp.int32)]
        + [V((tok + tok // 2, feats), bf), V((feats, tok + tok // 2), bf)]
        + [V((heads, tok, HEAD_DIM), bf)] * 4
        + [V((heads, 2 * tok, HEAD_DIM), bf)] * 2
        + [V((heads, tok, tok), f32)] * 2
        + [V((heads, 8, lanes), f32)] * 4
        + [V((heads, tok + tok // 2, HEAD_DIM), f32)]
        + [V((heads, tok // 2, HEAD_DIM), bf)] * 2
        + [V((CORES, YN, part, w), bf) for w in wide]
        + [V((YN, part, w), bf) for w in wide]
        + [V((YN, part, w), bf) for w in wide]
        + [V((xn - 1, part, w), bf) for w in wide]
        + [V((half, rows, w), f32) for w in wide]
        + [V((ZN - 1, rows, w), f32) for w in wide]
        + [V((rows, w), f32) for w in wide]
        + [V((ys - 1, rows, w), f32) for w in wide]
        + [V((rows, w), f32) for w in wide]
        + [dma((4, heads)), dma((1,)), dma((1,))]
        + [dma((4, heads))] * 2
        + [dma((1,))] * 2
        + [dma((1,))] * 2
        + [dma((heads,))] * 4
        + [dma((nu,))] * 2
        + [dma((nu, xn - 1))] * 2
        + [dma((nu, half)), dma((nu, ZN - 1))]
        + [dma((nu, YH)), dma((nu, ys - 1))]
        + [dma((nu, xn, CORES)), dma((nu,))]
    )
    gradient = pl.pallas_call(
        kernel,
        out_shape=jax.ShapeDtypeStruct((rows, width), f32),
        in_specs=[pl.BlockSpec(memory_space=pltpu.HBM)] * 6,
        out_specs=pl.BlockSpec(memory_space=pltpu.VMEM),
        scratch_shapes=scratch,
        compiler_params=pltpu.CompilerParams(
            collective_id=0, has_side_effects=True, vmem_limit_bytes=VMEM_BYTES
        ),
        cost_estimate=pl.CostEstimate(flops=2_000_000_000, bytes_accessed=3_000_000, transcendentals=2_000_000),
    )(inputs, query_states, key_states, value_states, out_grad, first_flags)
    return adamw(weight, moment_one, moment_two, gradient)


def solution(mesh):
    in_specs = (
        P("clip", "tm", None),
        P("clip", "tm", None),
        P("clip", "tm", None),
        P("clip", "tm", None),
        P("clip", "tm", None),
        P("clip", None),
        P("tm", None),
        P("tm", None),
        P("tm", None),
    )
    out_specs = (P("tm", None), P("tm", None), P("tm", None))
    return jax.shard_map(body, mesh=mesh, in_specs=in_specs, out_specs=out_specs, check_vma=False)
```

time: 92.8 us -> 77.2 us (0.83)
  the two profiles are of different devices: /device:TPU:57 before, /device:TPU:5 now
where the time goes in v2:
time: 77.2 us; the launch traced here: 77 us
  Pallas kernels  74.7 us (97%)
  other arithmetic  1.59 us (2%)
    pallas_call x1, Pallas kernels, body(): pl.pallas_call(kernel, out_shape=jax.ShapeDtypeStruct((rows, width), f32)...  74.7 us
    sub x1, other arithmetic, adamw(): weight - learn_rate * (corr_one / (jnp.sqrt(corr_two) + adam_eps) + decay...  1.59 us

profile of v2, /device:TPU:5, one launch (start us, length us, event | category | flops | bytes accessed | tf_op | source)
XLA Modules:
  0.0 77.0 jit_solution(11765249125089399220)
XLA Ops:
  0.6 0.0 copy-start.2
  0.6 0.0 copy-start.1
  0.7 0.0 copy-start
  0.7 74.7 %shard_map.112 = f32[24,768]{1,0:T(8,128)} custom-call(bf16[1,320,768]{2,1,0:T(8,128)(2,1)} %x_hbm.1, bf16[1,320,768]{2,1,0:T(8,128)(2,1)} %q_hbm.1, bf16[1,320,768]{2,1,0:T(8,128)(2,1)} %k_hbm.1, bf16[1,320,768]{2,1,0:T(8,128)(2,1)} %v_hbm.1, bf16[1,320,768]{2,1,0:T(8,128)(2,1)} %g_hbm.1, s32[1,32]{1,0:T(1,128)} %flags_hbm.1), custom_call_target="tpu_custom_call" | custom-call | flops 2000000000 | bytes 3000000 | tf_op jit(solution)/shard_map/pallas_call | solution.py:534
  75.4 0.0 copy-done.2
  75.4 0.0 copy-done.1
  75.4 0.0 copy-done
  75.4 1.6 %multiply_subtract_fusion = (f32[24,768]{1,0:T(8,128)}, f32[24,768]{1,0:T(8,128)}, f32[24,768]{1,0:T(8,128)}) fusion(f32[24,768]{1,0:T(8,128)S(1)} %copy-done, f32[24,768]{1,0:T(8,128)} %shard_map.112, f32[24,768]{1,0:T(8,128)S(1)} %copy-done.1, f32[24,768]{1,0:T(8,128)S(1)} %copy-done.2), kind=kLoop, calls=%fused_computation.2 | loop fusion | flops 276480 | bytes 516096 | tf_op jit(solution)/shard_map/sub | solution.py:35
Async XLA Ops:
  0.6 74.7 %copy-start.2 = (f32[24,768]{1,0:T(8,128)S(1)}, f32[24,768]{1,0:T(8,128)}, u32[]{:S(2)}) copy-start(f32[24,768]{1,0:T(8,128)} %param.17) | copy-start | bytes 221188
  0.6 74.7 %copy-start.1 = (f32[24,768]{1,0:T(8,128)S(1)}, f32[24,768]{1,0:T(8,128)}, u32[]{:S(2)}) copy-start(f32[24,768]{1,0:T(8,128)} %param.16) | copy-start | bytes 221188
  0.7 74.7 %copy-start = (f32[24,768]{1,0:T(8,128)S(1)}, f32[24,768]{1,0:T(8,128)}, u32[]{:S(2)}) copy-start(f32[24,768]{1,0:T(8,128)} %param.15) | copy-start | bytes 221188

commit v3 on v2

--- a/solution.py
+++ b/solution.py
@@ -17,6 +17,7 @@
 YN = 4
 YH = 2
 CORES = 2
+ROUNDS = 3
 UNITS = ((0, 2), (2, 4), (4, 5), (5, 6))
 
 beta_one = 0.9
@@ -56,7 +57,7 @@
     nu = len(UNITS)
     gbuf, a_in, abuf, b_in, bbuf, c_in, cbuf, y_in, d_in = [rest[i * nu : (i + 1) * nu] for i in range(9)]
     (sem_loc, sem_locx, sem_f, win_s, win_r, x_s, x_r, os_s, os_r, nf_s, nf_r,
-     ret_s, ret_r, a_s, a_r, b_s, b_r, c_s, c_r, y_s, y_r, d_s, d_r) = rest[9 * nu :]
+     near_sem, ret_s, ret_r, a_s, a_r, b_s, b_r, c_s, c_r, y_s, y_r, d_s, d_r) = rest[9 * nu :]
     heads, tok, _ = qo.shape
     half = ZN // CORES
     rows = grad_out.shape[0]
@@ -172,10 +173,6 @@
     def start_local(h):
         for cp in local_copies(h):
             cp.start()
-    each(0, heads, start_local)
-    x_local.start()
-    f_local.start()
-
     bar = pltpu.get_barrier_semaphore()
     def hello(where):
         pl.semaphore_signal(bar, inc=1, device_id=where, device_id_type=MESH)
@@ -186,12 +183,25 @@
     def _():
         hello({"tm": nxt})
     hello({"clip": sibling})
-    each(1, ys, lambda d: hello(at_y(lax.rem(y + d, ys))))
-    each(1, ZN, lambda d: hello(at_z(lax.rem(z + d, ZN))))
-    for k in range(CORES):
-        each(1, xn, lambda d: hello(at_x(d, k)))
-    count = 1 + (ys - 1) + (ZN - 1) + CORES * (xn - 1)
+    beside = [
+        at_z(lax.rem(z + 1, ZN)), at_z(lax.rem(z + ZN - 1, ZN)),
+        at_y(lax.rem(y + 1, ys)), at_y(lax.rem(y + ys - 1, ys)),
+        at_x(1, core), at_x(xn - 1, core),
+    ]
+    for where in beside:
+        hello(where)
+    count = 1 + len(beside)
+    each(0, heads, start_local)
+    x_local.start()
+    f_local.start()
     pl.semaphore_wait(bar, count + has_prev.astype(jnp.int32) + has_next.astype(jnp.int32))
+
+    def tell(i):
+        for where in beside:
+            pl.semaphore_signal(near_sem.at[i], inc=1, device_id=where, device_id_type=MESH)
+
+    def hear(i):
+        pl.semaphore_wait(near_sem.at[i], len(beside))
 
     def send_window(h):
         @pl.when(has_next)
@@ -208,6 +218,7 @@
     def _():
         x_copy.start()
     send_window(1)
+    tell(0)
 
     @pl.when(jnp.logical_not(has_prev))
     def _():
@@ -260,9 +271,7 @@
     @pl.when(has_prev)
     def _():
         os_copy.start()
-    @pl.when(has_next)
-    def _():
-        os_copy.wait_recv()
+    send_window(2)
 
     f_local.wait()
     fo = flags[0, t]
@@ -278,9 +287,6 @@
         return fa, fb, inv, (fa * da + fb * db) * inv
 
     def near_far(h):
-        @pl.when(h + 2 < heads)
-        def _():
-            send_window(h + 2)
         @pl.when(has_prev)
         def _():
             for cp in ahead(h):
@@ -306,6 +312,9 @@
         @pl.when(has_next)
         def _():
             nf_copy(h).start()
+        @pl.when(jnp.logical_and(h == 0, has_next))
+        def _():
+            os_copy.wait_recv()
         ma, la, da = get(own_st_in, h)
         _, fb, inv, delta = total(ma, la, da, mb, lb, db)
         w = fb * inv * scaling
@@ -317,19 +326,22 @@
         @pl.when(has_prev)
         def _():
             ret_copy(h).start()
+        @pl.when(h + 3 < heads)
+        def _():
+            send_window(h + 3)
 
     def finish(h):
         @pl.when(has_prev)
         def _():
             nf_copy(h).wait_recv()
-        @pl.when(has_next)
-        def _():
-            ret_copy(h).wait_recv()
         ma, la, da = get(own_st, h)
         mb, lb, db = get(nf_st_in, h)
         fa, _, inv, delta = total(ma, la, da, mb, lb, db)
         ds = ((e_own[h] * (fa * inv * scaling)) * (dp_own[h] - delta)).astype(bf)
         own = dot_nn(ds, qo[h])
+        @pl.when(has_next)
+        def _():
+            ret_copy(h).wait_recv()
         back = ret_in[h].astype(f32)
         kg = jnp.concatenate(
             [kgn[h, 0:cut] + own[:cut], kgn[h, cut:tok] + own[cut:] + back, kgn[h, tok : tok + cut]], axis=0
@@ -411,6 +423,12 @@
         @pl.when(h > 0)
         def _():
             finish(h - 1)
+        @pl.when(h < ROUNDS)
+        def _():
+            hear(h)
+        @pl.when(h < ROUNDS - 1)
+        def _():
+            tell(h + 1)
         @pl.when(h == 2)
         def _():
             a_copy(0).start()
@@ -424,64 +442,87 @@
         def _():
             a_copy(2).start()
             a_finish(1)
-            b_finish(0)
         return carry
     lax.fori_loop(0, heads + 1, main, 0)
 
-    a_copy(3).start()
-    b_finish(1)
-    c_finish(0)
-    a_finish(3)
-    b_finish(2)
-    y_finish(0)
-    c_finish(1)
-    b_finish(3)
-    c_finish(2)
-    y_finish(1)
-    c_finish(3)
-    y_finish(2)
-    d_finish(0)
-    d_finish(1)
-    y_finish(3)
-    d_finish(2)
-    d_finish(3)
-
-    @pl.when(has_next)
-    def _():
-        x_copy.wait_send()
-        def sent(h):
-            for cp in ahead(h):
-                cp.wait_send()
-            nf_copy(h).wait_send()
-        each(0, heads, sent)
-    @pl.when(has_prev)
-    def _():
-        os_copy.wait_send()
-        def sent(h):
-            for cp in behind(h):
-                cp.wait_send()
-            ret_copy(h).wait_send()
-        each(0, heads, sent)
-    for u in range(nu):
+    def sent_window():
+        @pl.when(has_next)
+        def _():
+            x_copy.wait_send()
+            def sent(h):
+                for cp in ahead(h):
+                    cp.wait_send()
+                nf_copy(h).wait_send()
+            each(0, heads, sent)
+        @pl.when(has_prev)
+        def _():
+            os_copy.wait_send()
+            def sent(h):
+                for cp in behind(h):
+                    cp.wait_send()
+                ret_copy(h).wait_send()
+            each(0, heads, sent)
+
+    def sent_ab(u):
         a_copy(u).wait_send()
         each(1, xn, lambda d: b_copy(u, d).wait_send())
+
+    def sent_c(u):
         def left(i):
             @pl.when(core * half + i != z)
             def _():
                 c_copy(u, i).wait_send()
         each(0, half, left)
+
+    def sent_y(u):
         @pl.when(holder)
         def _():
-            def left_y(k):
+            def left(k):
                 @pl.when(x + k * YN != y)
                 def _():
                     y_copy(u, k).wait_send()
-            each(0, YH, left_y)
+            each(0, YH, left)
+
+    def sent_d(u):
         @pl.when(final)
         def _():
             d_near(u).wait_send()
             for k in range(CORES):
                 each(1, xn, lambda d: d_copy(u, d, k).wait_send())
+
+    last = nu - 1
+    a_copy(last).start()
+    sent_window()
+    b_finish(0)
+    b_finish(1)
+    a_finish(last)
+    b_finish(2)
+    for u in range(last):
+        sent_ab(u)
+    c_finish(0)
+    c_finish(1)
+    b_finish(last)
+    c_finish(2)
+    sent_ab(last)
+    for u in range(last):
+        sent_c(u)
+    y_finish(0)
+    y_finish(1)
+    c_finish(last)
+    y_finish(2)
+    for u in range(last):
+        sent_y(u)
+    d_finish(0)
+    d_finish(1)
+    sent_d(0)
+    sent_d(1)
+    sent_c(last)
+    y_finish(last)
+    d_finish(2)
+    sent_d(2)
+    sent_y(last)
+    d_finish(last)
+    sent_d(last)
 
 
 def body(
@@ -524,7 +565,9 @@
         + [dma((4, heads))] * 2
         + [dma((1,))] * 2
         + [dma((1,))] * 2
-        + [dma((heads,))] * 4
+        + [dma((heads,))] * 2
+        + [pltpu.SemaphoreType.REGULAR((ROUNDS,))]
+        + [dma((heads,))] * 2
         + [dma((nu,))] * 2
         + [dma((nu, xn - 1))] * 2
         + [dma((nu, half)), dma((nu, ZN - 1))]

time: 77.2 us -> 74.2 us (0.961)
  the two profiles are of different devices: /device:TPU:5 before, /device:TPU:17 now
where the time goes in v3:
time: 74.2 us; the launch traced here: 74 us
  Pallas kernels  71.7 us (97%)
  other arithmetic  1.59 us (2%)
    pallas_call x1, Pallas kernels, body(): pl.pallas_call(kernel, out_shape=jax.ShapeDtypeStruct((rows, width), f32)...  71.7 us
    sub x1, other arithmetic, adamw(): weight - learn_rate * (corr_one / (jnp.sqrt(corr_two) + adam_eps) + decay...  1.59 us

profile of v3, /device:TPU:17, one launch (start us, length us, event | category | flops | bytes accessed | tf_op | source)
XLA Modules:
  0.0 74.0 jit_solution(15384653761257176188)
XLA Ops:
  0.6 0.0 copy-start.2
  0.6 0.0 copy-start.1
  0.7 0.0 copy-start
  0.7 71.7 %shard_map.112 = f32[24,768]{1,0:T(8,128)} custom-call(bf16[1,320,768]{2,1,0:T(8,128)(2,1)} %x_hbm.1, bf16[1,320,768]{2,1,0:T(8,128)(2,1)} %q_hbm.1, bf16[1,320,768]{2,1,0:T(8,128)(2,1)} %k_hbm.1, bf16[1,320,768]{2,1,0:T(8,128)(2,1)} %v_hbm.1, bf16[1,320,768]{2,1,0:T(8,128)(2,1)} %g_hbm.1, s32[1,32]{1,0:T(1,128)} %flags_hbm.1), custom_call_target="tpu_custom_call" | custom-call | flops 2000000000 | bytes 3000000 | tf_op jit(solution)/shard_map/pallas_call | solution.py:577
  72.4 0.0 copy-done.2
  72.4 0.0 copy-done.1
  72.4 0.0 copy-done
  72.4 1.6 %multiply_subtract_fusion = (f32[24,768]{1,0:T(8,128)}, f32[24,768]{1,0:T(8,128)}, f32[24,768]{1,0:T(8,128)}) fusion(f32[24,768]{1,0:T(8,128)S(1)} %copy-done, f32[24,768]{1,0:T(8,128)} %shard_map.112, f32[24,768]{1,0:T(8,128)S(1)} %copy-done.1, f32[24,768]{1,0:T(8,128)S(1)} %copy-done.2), kind=kLoop, calls=%fused_computation.2 | loop fusion | flops 276480 | bytes 516096 | tf_op jit(solution)/shard_map/sub | solution.py:36
Async XLA Ops:
  0.6 71.8 %copy-start.2 = (f32[24,768]{1,0:T(8,128)S(1)}, f32[24,768]{1,0:T(8,128)}, u32[]{:S(2)}) copy-start(f32[24,768]{1,0:T(8,128)} %param.17) | copy-start | bytes 221188
  0.6 71.8 %copy-start.1 = (f32[24,768]{1,0:T(8,128)S(1)}, f32[24,768]{1,0:T(8,128)}, u32[]{:S(2)}) copy-start(f32[24,768]{1,0:T(8,128)} %param.16) | copy-start | bytes 221188
  0.7 71.8 %copy-start = (f32[24,768]{1,0:T(8,128)S(1)}, f32[24,768]{1,0:T(8,128)}, u32[]{:S(2)}) copy-start(f32[24,768]{1,0:T(8,128)} %param.15) | copy-start | bytes 221188

commit v4 on v3

--- a/solution.py
+++ b/solution.py
@@ -84,7 +84,7 @@
     def cols(h):
         return pl.ds(pl.multiple_of(h * HEAD_DIM, HEAD_DIM), HEAD_DIM)
 
-    cut = tok // 2
+    cut = tok * 2 // 5
     own_rows = pl.ds(0, tok)
     prev_rows = pl.ds(tok, tok)
 
@@ -541,17 +541,18 @@
     nu = len(UNITS)
     bf, f32 = jnp.bfloat16, jnp.float32
     V = pltpu.VMEM
+    cut = tok * 2 // 5
     lanes = (tok + 127) // 128 * 128
     dma = pltpu.SemaphoreType.DMA
     scratch = (
         [pltpu.SMEM(first_flags.shape, jnp.int32)]
-        + [V((tok + tok // 2, feats), bf), V((feats, tok + tok // 2), bf)]
+        + [V((tok + cut, feats), bf), V((feats, tok + cut), bf)]
         + [V((heads, tok, HEAD_DIM), bf)] * 4
         + [V((heads, 2 * tok, HEAD_DIM), bf)] * 2
         + [V((heads, tok, tok), f32)] * 2
         + [V((heads, 8, lanes), f32)] * 4
-        + [V((heads, tok + tok // 2, HEAD_DIM), f32)]
-        + [V((heads, tok // 2, HEAD_DIM), bf)] * 2
+        + [V((heads, tok + cut, HEAD_DIM), f32)]
+        + [V((heads, tok - cut, HEAD_DIM), bf)] * 2
         + [V((CORES, YN, part, w), bf) for w in wide]
         + [V((YN, part, w), bf) for w in wide]
         + [V((YN, part, w), bf) for w in wide]

time: 74.2 us -> 74 us (level)
  the two profiles are of different devices: /device:TPU:17 before, /device:TPU:5 now
where the time goes in v4:
time: 74 us; the launch traced here: 73.9 us
  Pallas kernels  71.6 us (97%)
  other arithmetic  1.59 us (2%)
    pallas_call x1, Pallas kernels, body(): pl.pallas_call(kernel, out_shape=jax.ShapeDtypeStruct((rows, width), f32)...  71.6 us
    sub x1, other arithmetic, adamw(): weight - learn_rate * (corr_one / (jnp.sqrt(corr_two) + adam_eps) + decay...  1.59 us

profile of v4, /device:TPU:5, one launch (start us, length us, event | category | flops | bytes accessed | tf_op | source)
XLA Modules:
  0.0 73.9 jit_solution(17526900728575253616)
XLA Ops:
  0.6 0.0 copy-start.2
  0.6 0.0 copy-start.1
  0.7 0.0 copy-start
  0.7 71.6 %shard_map.112 = f32[24,768]{1,0:T(8,128)} custom-call(bf16[1,320,768]{2,1,0:T(8,128)(2,1)} %x_hbm.1, bf16[1,320,768]{2,1,0:T(8,128)(2,1)} %q_hbm.1, bf16[1,320,768]{2,1,0:T(8,128)(2,1)} %k_hbm.1, bf16[1,320,768]{2,1,0:T(8,128)(2,1)} %v_hbm.1, bf16[1,320,768]{2,1,0:T(8,128)(2,1)} %g_hbm.1, s32[1,32]{1,0:T(1,128)} %flags_hbm.1), custom_call_target="tpu_custom_call" | custom-call | flops 2000000000 | bytes 3000000 | tf_op jit(solution)/shard_map/pallas_call | solution.py:578
  72.2 0.0 copy-done.2
  72.2 0.0 copy-done.1
  72.3 0.0 copy-done
  72.3 1.6 %multiply_subtract_fusion = (f32[24,768]{1,0:T(8,128)}, f32[24,768]{1,0:T(8,128)}, f32[24,768]{1,0:T(8,128)}) fusion(f32[24,768]{1,0:T(8,128)S(1)} %copy-done, f32[24,768]{1,0:T(8,128)} %shard_map.112, f32[24,768]{1,0:T(8,128)S(1)} %copy-done.1, f32[24,768]{1,0:T(8,128)S(1)} %copy-done.2), kind=kLoop, calls=%fused_computation.2 | loop fusion | flops 276480 | bytes 516096 | tf_op jit(solution)/shard_map/sub | solution.py:36
Async XLA Ops:
  0.6 71.6 %copy-start.2 = (f32[24,768]{1,0:T(8,128)S(1)}, f32[24,768]{1,0:T(8,128)}, u32[]{:S(2)}) copy-start(f32[24,768]{1,0:T(8,128)} %param.17) | copy-start | bytes 221188
  0.6 71.6 %copy-start.1 = (f32[24,768]{1,0:T(8,128)S(1)}, f32[24,768]{1,0:T(8,128)}, u32[]{:S(2)}) copy-start(f32[24,768]{1,0:T(8,128)} %param.16) | copy-start | bytes 221188
  0.7 71.6 %copy-start = (f32[24,768]{1,0:T(8,128)S(1)}, f32[24,768]{1,0:T(8,128)}, u32[]{:S(2)}) copy-start(f32[24,768]{1,0:T(8,128)} %param.15) | copy-start | bytes 221188

commit v5 on v4

--- a/solution.py
+++ b/solution.py
@@ -499,30 +499,26 @@
     b_finish(2)
     for u in range(last):
         sent_ab(u)
+    b_finish(last)
     c_finish(0)
     c_finish(1)
-    b_finish(last)
     c_finish(2)
     sent_ab(last)
     for u in range(last):
         sent_c(u)
+    c_finish(last)
     y_finish(0)
     y_finish(1)
-    c_finish(last)
     y_finish(2)
+    sent_c(last)
     for u in range(last):
         sent_y(u)
-    d_finish(0)
-    d_finish(1)
-    sent_d(0)
-    sent_d(1)
-    sent_c(last)
     y_finish(last)
-    d_finish(2)
-    sent_d(2)
     sent_y(last)
-    d_finish(last)
-    sent_d(last)
+    for u in range(nu):
+        d_finish(u)
+    for u in range(nu):
+        sent_d(u)
 
 
 def body(

time: 74 us -> 71.6 us (0.968)
  Pallas kernels: 71.6 us -> 69.1 us
    pallas_call x1, Pallas kernels: 71.6 us -> 69.1 us  [body(): pl.pallas_call(kernel, out_shape=jax.ShapeDtypeStruct((rows, width), f32)...]
where the time goes in v5:
time: 71.6 us; the launch traced here: 71.4 us
  Pallas kernels  69.1 us (97%)
  other arithmetic  1.59 us (2%)
    pallas_call x1, Pallas kernels, body(): pl.pallas_call(kernel, out_shape=jax.ShapeDtypeStruct((rows, width), f32)...  69.1 us
    sub x1, other arithmetic, adamw(): weight - learn_rate * (corr_one / (jnp.sqrt(corr_two) + adam_eps) + decay...  1.59 us

profile of v5, /device:TPU:5, one launch (start us, length us, event | category | flops | bytes accessed | tf_op | source)
XLA Modules:
  0.0 71.4 jit_solution(8367448640285841778)
XLA Ops:
  0.6 0.0 copy-start.2
  0.6 0.0 copy-start.1
  0.7 0.0 copy-start
  0.7 69.1 %shard_map.112 = f32[24,768]{1,0:T(8,128)} custom-call(bf16[1,320,768]{2,1,0:T(8,128)(2,1)} %x_hbm.1, bf16[1,320,768]{2,1,0:T(8,128)(2,1)} %q_hbm.1, bf16[1,320,768]{2,1,0:T(8,128)(2,1)} %k_hbm.1, bf16[1,320,768]{2,1,0:T(8,128)(2,1)} %v_hbm.1, bf16[1,320,768]{2,1,0:T(8,128)(2,1)} %g_hbm.1, s32[1,32]{1,0:T(1,128)} %flags_hbm.1), custom_call_target="tpu_custom_call" | custom-call | flops 2000000000 | bytes 3000000 | tf_op jit(solution)/shard_map/pallas_call | solution.py:574
  69.8 0.0 copy-done.2
  69.8 0.0 copy-done.1
  69.8 0.0 copy-done
  69.8 1.6 %multiply_subtract_fusion = (f32[24,768]{1,0:T(8,128)}, f32[24,768]{1,0:T(8,128)}, f32[24,768]{1,0:T(8,128)}) fusion(f32[24,768]{1,0:T(8,128)S(1)} %copy-done, f32[24,768]{1,0:T(8,128)} %shard_map.112, f32[24,768]{1,0:T(8,128)S(1)} %copy-done.1, f32[24,768]{1,0:T(8,128)S(1)} %copy-done.2), kind=kLoop, calls=%fused_computation.2 | loop fusion | flops 276480 | bytes 516096 | tf_op jit(solution)/shard_map/sub | solution.py:36
Async XLA Ops:
  0.6 69.2 %copy-start.2 = (f32[24,768]{1,0:T(8,128)S(1)}, f32[24,768]{1,0:T(8,128)}, u32[]{:S(2)}) copy-start(f32[24,768]{1,0:T(8,128)} %param.17) | copy-start | bytes 221188
  0.6 69.2 %copy-start.1 = (f32[24,768]{1,0:T(8,128)S(1)}, f32[24,768]{1,0:T(8,128)}, u32[]{:S(2)}) copy-start(f32[24,768]{1,0:T(8,128)} %param.16) | copy-start | bytes 221188
  0.7 69.2 %copy-start = (f32[24,768]{1,0:T(8,128)S(1)}, f32[24,768]{1,0:T(8,128)}, u32[]{:S(2)}) copy-start(f32[24,768]{1,0:T(8,128)} %param.15) | copy-start | bytes 221188
